TPU v7x, 256 devices: a whole 4x4x8 slice. The times are simulated.
256 devices in a mesh: section: 8 (over z), seq: 32 (over x, y, core).
Axes of the slice: x: 4, y: 4, z: 8, core: 2. Of those that a mesh axis runs over, the one named last changes fastest.
Arguments:
- patch_qkv: bfloat16 [16, 2, 32, 3, 16384], P('section', None, None, None, 'seq'), may hold values from -12 to 12
- kv_cache: bfloat16 [16, 2, 32, 2, 65536], P('section', None, 'seq'), may hold values from -12 to 12
- text_kv: bfloat16 [16, 2, 32, 2, 21312], P('section', None, 'seq'), may hold values from -12 to 12
- entering: bfloat16 [8, 2, 32, 16384], P('section', None, None, 'seq'), may hold values from -6 to 6
- gates: float32 [16, 2, 32], P('section'), may hold values from 0.3 to 3
- block_split: int32 [8], P('section'), may hold values from 1 to 2
- patch_index: int32 [8], P('section'), may hold values from 0 to 3
Outputs:
- new_cache: bfloat16 [16, 2, 32, 2, 65536], P('section', None, 'seq')
- attended: bfloat16 [16, 2, 32, 16384], P('section', None, 'seq')
- handed: bfloat16 [8, 2, 32, 16384], P('section', None, None, 'seq')
All inputs are finite; a program needn't handle non-finite values.
Results may differ from a plain program's by a relative error of at most 0.006.
Values may be sent and summed in bfloat16 or wider, within the bound.
A program may use at most 64 MiB of HBM per device.

v0:
```python
import math

import jax
import jax.numpy as jnp
from jax import lax
from jax.experimental import pallas as pl
from jax.experimental.pallas import tpu as pltpu
from jax.sharding import PartitionSpec as P

HD = 64
PATCHES = 4
TXT = 333
SEQ = 32
PAIRS = 128
ROWS = 512
STALE = 384
TROWS = 176
LG = 4
MESH = pl.DeviceIdType.MESH
BF = jnp.bfloat16
F32 = jnp.float32
FACTOR = HD ** (-0.5) * math.log2(math.e)


def low_rows(shape):
    return lax.broadcasted_iota(jnp.int32, shape, len(shape) - 2) < 4


def low_lanes(shape):
    return lax.broadcasted_iota(jnp.int32, shape, len(shape) - 1) < HD


def split_pieces(x):
    pieces = x.astype(F32).reshape(16, 2, 2, 8, 128)
    even, odd = pieces[:, 0], pieces[:, 1]
    even, odd = even.reshape(32, 8, 128), odd.reshape(32, 8, 128)
    mask = low_rows(even.shape)
    first = jnp.where(mask, even, pltpu.roll(odd, 4, 1)).reshape(16, 2, 8, 128)
    second = jnp.where(mask, pltpu.roll(even, 4, 1), odd).reshape(16, 2, 8, 128)
    return [
        half[:, layer].reshape(PAIRS, 128) for layer in range(2) for half in (first, second)
    ]


def kernel(
    patch_ref, split_ref, gates_ref, qkv_hbm, kv_hbm, text_hbm, ent_hbm,
    cache_hbm, att_hbm, hand_hbm,
    qkv_v, kv_v, text_v, ent_v, stage, tstage, send_q, send_kv, recv_q, recv_kv,
    keys, values, queries, maxima, partial,
    att_v, send_b, recv_b, hand_v,
    load_sem, q_send, q_recv, kv_send, kv_recv, e_send, e_recv, b_send, b_recv, out_sem,
):
    sections = lax.axis_size("section")
    sec = lax.axis_index("section")
    me = lax.axis_index("seq")
    after = lax.rem(sec + 1, sections)
    before = lax.rem(sec + sections - 1, sections)

    load_qkv = pltpu.make_async_copy(qkv_hbm, qkv_v, load_sem.at[0])
    load_kv = pltpu.make_async_copy(kv_hbm, kv_v, load_sem.at[1])
    load_text = pltpu.make_async_copy(text_hbm, text_v, load_sem.at[2])
    load_qkv.start()
    load_kv.start()
    load_text.start()

    barrier = pltpu.get_barrier_semaphore()

    def greet(step, carry):
        other = lax.rem(me + step, SEQ)
        pl.semaphore_signal(barrier, inc=1, device_id=(sec, other), device_id_type=MESH)
        return carry

    def greet_before(step, carry):
        other = lax.rem(me + step, SEQ)
        pl.semaphore_signal(barrier, inc=1, device_id=(before, other), device_id_type=MESH)
        return carry

    lax.fori_loop(1, SEQ, greet, 0)
    lax.fori_loop(0, SEQ, greet_before, 0)

    def arrange(part):
        for lg in range(LG):
            rows = qkv_v[lg * 3 + part].astype(F32)
            for at in range(4):
                stage[pl.ds(lg * 4 + at, SEQ, stride=16), :] = rows[:, at * 128:(at + 1) * 128]
        return stage[...].reshape(SEQ, 16, 128).astype(BF)

    load_qkv.wait()
    send_q[...] = arrange(0)
    pl.semaphore_wait(barrier, 2 * SEQ - 1)

    def q_copy(other):
        return pltpu.make_async_remote_copy(
            src_ref=send_q.at[other], dst_ref=recv_q.at[me], send_sem=q_send, recv_sem=q_recv,
            device_id=(sec, other), device_id_type=MESH,
        )

    def kv_copy(other):
        return pltpu.make_async_remote_copy(
            src_ref=send_kv.at[other], dst_ref=recv_kv.at[me], send_sem=kv_send, recv_sem=kv_recv,
            device_id=(sec, other), device_id_type=MESH,
        )

    def b_copy(other):
        return pltpu.make_async_remote_copy(
            src_ref=send_b.at[other], dst_ref=recv_b.at[me], send_sem=b_send, recv_sem=b_recv,
            device_id=(after, other), device_id_type=MESH,
        )

    def send_queries(step, carry):
        q_copy(lax.rem(me + step, SEQ)).start()
        return carry

    def send_pairs(step, carry):
        kv_copy(lax.rem(me + step, SEQ)).start()
        return carry

    def send_branch(step, carry):
        b_copy(lax.rem(me + step, SEQ)).start()
        return carry

    lax.fori_loop(1, SEQ, send_queries, 0)
    pltpu.make_async_copy(send_q.at[me], recv_q.at[me], q_recv).start()
    send_kv[:, :, 0:128] = arrange(1)
    send_kv[:, :, 128:256] = arrange(2)
    lax.fori_loop(1, SEQ, send_pairs, 0)
    pltpu.make_async_copy(send_kv.at[me], recv_kv.at[me], kv_recv).start()
    ent_copy = pltpu.make_async_remote_copy(
        src_ref=ent_hbm, dst_ref=ent_v, send_sem=e_send, recv_sem=e_recv,
        device_id=(after, me), device_id_type=MESH,
    )
    ent_copy.start()

    load_kv.wait()
    load_text.wait()

    slots = jnp.full((PAIRS, 128), patch_ref[0], jnp.int32)
    counts = jnp.full((PAIRS, 128), split_ref[0], jnp.int32)

    def prepare(lg, carry):
        tstage[...] = kv_v[lg].astype(F32)
        for at in range(PATCHES - 1):
            ahead = at < slots
            rows = pl.ds(at * PAIRS, PAIRS)
            here, later = at * 256, (at + 1) * 256
            keys[lg, rows, :] = jnp.where(
                ahead,
                tstage[pl.ds(here, PAIRS, stride=2), :],
                tstage[pl.ds(later, PAIRS, stride=2), :],
            ).astype(BF)
            values[lg, rows, 0:128] = jnp.where(
                ahead,
                tstage[pl.ds(here + 1, PAIRS, stride=2), :],
                tstage[pl.ds(later + 1, PAIRS, stride=2), :],
            ).astype(BF)
        values[lg, 0:STALE, 128:256] = jnp.ones((STALE, 128), BF)
        for at in range(TXT // 2):
            tstage[2 * at:2 * at + 2, :] = text_v[lg, :, at * 128:(at + 1) * 128].astype(F32)
        last = text_v[lg, :, TXT // 2 * 128:TXT * HD].astype(F32)
        last = jnp.concatenate([last, last], axis=1)
        row = lax.broadcasted_iota(jnp.int32, (TROWS, 128), 0)
        lane = lax.broadcasted_iota(jnp.int32, (TROWS, 128), 1)
        whole = row < TXT // 2
        half = (row == TXT // 2) & (lane < HD)
        keys[lg, STALE:, :] = jnp.where(whole, tstage[pl.ds(0, TROWS, stride=2), :], last[0:1]).astype(BF)
        end = jnp.where(half, last[1:2], 0.0)
        values[lg, STALE:, 0:128] = jnp.where(
            whole, tstage[pl.ds(1, TROWS, stride=2), :], end
        ).astype(BF)
        values[lg, STALE:, 128:256] = jnp.where(whole | half, 1.0, 0.0).astype(BF)
        return carry

    lax.fori_loop(0, LG, prepare, 0)

    pltpu.make_async_copy(recv_q, recv_q, q_recv).wait()
    lanes = low_lanes((PAIRS, 128))
    for lg, q in enumerate(split_pieces(recv_q[...])):
        turned = pltpu.roll(q, HD, 1)
        queries[lg, 0:128] = jnp.where(lanes, q, 0.0).astype(BF)
        queries[lg, 128:256] = jnp.where(lanes, turned, 0.0).astype(BF)
        queries[lg, 256:384] = jnp.where(lanes, 0.0, turned).astype(BF)
        queries[lg, 384:512] = jnp.where(lanes, 0.0, q).astype(BF)

    def scores_of(lg, k):
        return lax.dot_general(
            queries[lg], k, (((1,), (1,)), ((), ())), preferred_element_type=F32
        )

    def top(s):
        best = jnp.max(s, axis=1, keepdims=True)
        return jnp.maximum(best[0:256], best[256:512])

    def attend_stale(lg, carry):
        k = keys[lg]
        v = values[lg]
        s = scores_of(lg, k)
        best = top(s)
        maxima[lg] = jnp.broadcast_to(best, (256, 128))
        w = jnp.exp2((s - jnp.concatenate([best, best], axis=0)) * FACTOR).astype(BF)
        partial[lg] = jnp.dot(w, v, preferred_element_type=F32)
        return carry

    lax.fori_loop(0, LG, attend_stale, 0)

    pltpu.make_async_copy(recv_kv, recv_kv, kv_recv).wait()
    fresh_k = split_pieces(recv_kv[:, :, 0:128])
    fresh_v = split_pieces(recv_kv[:, :, 128:256])
    runs = [layer < counts for layer in range(2)]
    branch = [None, None]
    for lg in range(LG):
        layer, half = lg // 2, lg % 2
        tstage[pl.ds(0, PAIRS, stride=2), :] = fresh_k[lg]
        tstage[pl.ds(1, PAIRS, stride=2), :] = fresh_v[lg]
        for at in range(PATCHES * 2):
            here = runs[layer] & (slots == at // 2)
            rows = pl.ds(at * 128, 128)
            kv_v[lg, rows, :] = jnp.where(
                here, tstage[at % 2 * 128:(at % 2 + 1) * 128, :], kv_v[lg, rows, :].astype(F32)
            ).astype(BF)
        pltpu.make_async_copy(kv_v.at[lg], cache_hbm.at[lg], out_sem.at[0]).start()
    for lg in range(LG):
        layer, half = lg // 2, lg % 2
        s = scores_of(lg, fresh_k[lg].astype(BF))
        old = maxima[lg, :, 0:1]
        best = jnp.maximum(old, top(s))
        both = jnp.concatenate([best, best], axis=0)
        w = jnp.exp2((s - both) * FACTOR).astype(BF)
        v = jnp.concatenate([fresh_v[lg].astype(BF), jnp.ones((PAIRS, 128), BF)], axis=1)
        scale = jnp.exp2((old - best) * FACTOR)
        total = jnp.dot(w, v, preferred_element_type=F32)
        total = total + partial[lg] * jnp.concatenate([scale, scale], axis=0)

        def joined(part):
            a, b, c, d = (part[at * 128:(at + 1) * 128] for at in range(4))
            return jnp.where(lanes, a + pltpu.roll(c, HD, 1), pltpu.roll(b, HD, 1) + d)

        out = joined(total[:, 0:128]) / joined(total[:, 128:256])
        out = jnp.where(runs[layer], out, 0.0).astype(BF).astype(F32)
        stage[pl.ds(layer * 256 + half, PAIRS, stride=2), :] = out
        gated = gates_ref[layer, half, me] * out
        branch[half] = gated if branch[half] is None else branch[half] + gated

    first, second = (part.reshape(16, 8, 128) for part in branch)
    mask = low_rows(first.shape)
    even = jnp.where(mask, first, pltpu.roll(second, 4, 1))
    odd = jnp.where(mask, pltpu.roll(first, 4, 1), second)
    send_b[...] = jnp.stack([even, odd], axis=1).reshape(SEQ, 8, 128).astype(BF)
    lax.fori_loop(0, SEQ, send_branch, 0)
    att_v[...] = stage[...].astype(BF)
    store_att = pltpu.make_async_copy(att_v, att_hbm, out_sem.at[1])
    store_att.start()

    ent_copy.wait()
    pltpu.make_async_copy(recv_b, recv_b, b_recv).wait()
    tstage[0:256, :] = recv_b[...].astype(F32).reshape(256, 128)
    for half in range(2):
        for at in range(4):
            cols = pl.ds(at * 128, 128)
            moved = tstage[pl.ds(half * 4 + at, SEQ, stride=8), :]
            hand_v[half, :, cols] = (ent_v[half, :, cols].astype(F32) + moved).astype(BF)
    store_hand = pltpu.make_async_copy(hand_v, hand_hbm, out_sem.at[2])
    store_hand.start()

    pltpu.make_async_copy(send_b, send_b, b_send).wait()
    rest = pl.ds(0, SEQ - 1)
    pltpu.make_async_copy(send_q.at[rest], send_q.at[rest], q_send).wait()
    pltpu.make_async_copy(send_kv.at[rest], send_kv.at[rest], kv_send).wait()
    pltpu.make_async_copy(kv_v, cache_hbm, out_sem.at[0]).wait()
    store_att.wait()
    store_hand.wait()


def on_device(patch_qkv, kv_cache, text_kv, entering, gates, block_split, patch_index):
    qkv = jnp.transpose(patch_qkv, (0, 1, 3, 2, 4)).reshape(12, SEQ, 512)
    kv = kv_cache.reshape(LG, 2, ROWS, 128).transpose(0, 2, 1, 3).reshape(LG, 2 * ROWS, 128)
    text = text_kv.reshape(LG, 2, TXT * HD)
    ent = entering.reshape(2, SEQ, 512)
    hbm = pl.BlockSpec(memory_space=pl.ANY)
    smem = pl.BlockSpec(memory_space=pltpu.SMEM)
    vmem = pltpu.VMEM
    cache, att, handed = pl.pallas_call(
        kernel,
        out_shape=[
            jax.ShapeDtypeStruct((LG, 2 * ROWS, 128), BF),
            jax.ShapeDtypeStruct((4 * PAIRS, 128), BF),
            jax.ShapeDtypeStruct((2, SEQ, 512), BF),
        ],
        in_specs=[smem, smem, smem, hbm, hbm, hbm, hbm],
        out_specs=[hbm, hbm, hbm],
        scratch_shapes=[
            vmem((12, SEQ, 512), BF),
            vmem((LG, 2 * ROWS, 128), BF),
            vmem((LG, 2, TXT * HD), BF),
            vmem((2, SEQ, 512), BF),
            vmem((ROWS, 128), F32),
            vmem((2 * ROWS, 128), F32),
            vmem((SEQ, 16, 128), BF),
            vmem((SEQ, 16, 256), BF),
            vmem((SEQ, 16, 128), BF),
            vmem((SEQ, 16, 256), BF),
            vmem((LG, STALE + TROWS, 128), BF),
            vmem((LG, STALE + TROWS, 256), BF),
            vmem((LG, 4 * PAIRS, 128), BF),
            vmem((LG, 2 * PAIRS, 128), F32),
            vmem((LG, 4 * PAIRS, 256), F32),
            vmem((4 * PAIRS, 128), BF),
            vmem((SEQ, 8, 128), BF),
            vmem((SEQ, 8, 128), BF),
            vmem((2, SEQ, 512), BF),
            pltpu.SemaphoreType.DMA((3,)),
            pltpu.SemaphoreType.DMA,
            pltpu.SemaphoreType.DMA,
            pltpu.SemaphoreType.DMA,
            pltpu.SemaphoreType.DMA,
            pltpu.SemaphoreType.DMA,
            pltpu.SemaphoreType.DMA,
            pltpu.SemaphoreType.DMA,
            pltpu.SemaphoreType.DMA,
            pltpu.SemaphoreType.DMA((3,)),
        ],
        compiler_params=pltpu.CompilerParams(
            collective_id=0, has_side_effects=True, vmem_limit_bytes=56 * 1024 * 1024
        ),
    )(patch_index, block_split, gates, qkv, kv, text, ent)
    cache = cache.reshape(LG, ROWS, 2, 128).transpose(0, 2, 1, 3).reshape(kv_cache.shape)
    att = att.reshape(2, PAIRS, 2, 128).transpose(0, 2, 1, 3).reshape(2, 2, 1, 2 * PAIRS * HD)
    return cache, att, handed.reshape(entering.shape)


def solution(mesh):
    in_specs = (
        P("section", None, None, None, "seq"),
        P("section", None, "seq", None, None),
        P("section", None, "seq", None, None),
        P("section", None, None, "seq"),
        P("section", None, None),
        P("section"),
        P("section"),
    )
    out_specs = (
        P("section", None, "seq", None, None),
        P("section", None, "seq", None),
        P("section", None, None, "seq"),
    )
    return jax.shard_map(
        on_device, mesh=mesh, in_specs=in_specs, out_specs=out_specs, check_vma=False
    )
```

profile of v0, /device:TPU:1, one launch (start us, length us, event | category | flops | bytes accessed | tf_op | source)
XLA Modules:
  0.0 38.2 jit_solution(1389178911946168408)
XLA Ops:
  1.9 31.8 %shard_map.94 = (bf16[4,1024,128]{2,1,0:T(8,128)(2,1)}, bf16[512,128]{1,0:T(8,128)(2,1)}, bf16[2,32,512]{2,1,0:T(8,128)(2,1)}) custom-call(s32[1]{0:T(128)S(6)} %copy.17.patch_ref, s32[1]{0:T(128)S(6)} %copy.16.split_ref, f32[2,2,32]{2,1,0:T(2,128)} %gates_ref.1, bf16[12,32,512]{2,1,0:T(8,128)(2,1)} %bitcast.23, bf16[4,1024,128]{2,1,0:T(8,128)(2,1)} %bitcast.21, ...), custom_call_target="tpu_custom_call" | custom-call | tf_op jit(solution)/shard_map/pallas_call | solution.py:281
  33.7 0.0 copy-start
  33.7 2.9 %copy.18 = bf16[2,2,1,2,65536]{4,3,2,1,0:T(2,128)(2,1)} copy(bf16[2,2,1,2,65536]{4,3,2,1,0:T(2,128)(2,1)} %bitcast.22) | data formatting | bytes 2097152
  36.7 0.0 copy-done
  36.7 0.0 copy-start.1
  36.7 0.7 %copy.19 = bf16[2,2,1,16384]{3,1,2,0:T(2,128)(2,1)} copy(bf16[2,2,1,16384]{3,1,2,0:T(2,128)(2,1)S(1)} %bitcast.25) | data formatting | bytes 262144
  37.4 0.2 copy-done.1
  37.6 0.6 %copy.20 = bf16[1,2,32,512]{3,2,1,0:T(8,128)(2,1)} copy(bf16[1,2,32,512]{3,2,1,0:T(8,128)(2,1)S(1)} %bitcast.27) | data formatting | bytes 131072
Async XLA Ops:
  33.7 3.0 %copy-start = (bf16[512,128]{1,0:T(8,128)(2,1)S(1)}, bf16[512,128]{1,0:T(8,128)(2,1)}, u32[]{:S(2)}) copy-start(bf16[512,128]{1,0:T(8,128)(2,1)} %get-tuple-element.7) | copy-start | bytes 393220
  36.7 0.9 %copy-start.1 = (bf16[2,32,512]{2,1,0:T(8,128)(2,1)S(1)}, bf16[2,32,512]{2,1,0:T(8,128)(2,1)}, u32[]{:S(2)}) copy-start(bf16[2,32,512]{2,1,0:T(8,128)(2,1)} %get-tuple-element.8) | copy-start | bytes 196612
where the time goes:
time: 38.4 us; the launch traced here: 38.2 us
  Pallas kernels  31.8 us (83%)
  local copies, waits for them, and re-layouts  4.45 us (12%)
  between operations  1.94 us (5%)
    pallas_call x1, Pallas kernels, on_device(): pl.pallas_call(kernel, out_shape=[jax.ShapeDtypeStruct((LG, 2 * ROWS, 128...  31.8 us
    unnamed x7, local copies, waits for them, and re-layouts  4.45 us

commit v1 on v0

v1 whole, which is shorter than its diff:
```python
import math

import jax
import jax.numpy as jnp
from jax import lax
from jax.experimental import pallas as pl
from jax.experimental.pallas import tpu as pltpu
from jax.sharding import PartitionSpec as P

HD = 64
PATCHES = 4
TXT = 333
SEQ = 32
PAIRS = 128
ROWS = 512
STALE = 384
TROWS = 176
NKEY = STALE + TROWS
VROWS = 144
LG = 4
MESH = pl.DeviceIdType.MESH
BF = jnp.bfloat16
F32 = jnp.float32
FACTOR = HD ** (-0.5) * math.log2(math.e)


def far_first():
    hops = (0, 1, 2, 1)
    return sorted(range(1, SEQ), key=lambda flip: -(hops[flip // 8] + hops[flip // 2 % 4]))


def low_rows(shape):
    return lax.broadcasted_iota(jnp.int32, shape, len(shape) - 2) < 4


def split_pieces(x):
    pieces = x.astype(F32).reshape(16, 2, 2, 8, 128)
    even, odd = pieces[:, 0], pieces[:, 1]
    even, odd = even.reshape(32, 8, 128), odd.reshape(32, 8, 128)
    mask = low_rows(even.shape)
    first = jnp.where(mask, even, pltpu.roll(odd, 4, 1)).reshape(16, 2, 8, 128)
    second = jnp.where(mask, pltpu.roll(even, 4, 1), odd).reshape(16, 2, 8, 128)
    return [
        half[:, layer].reshape(PAIRS, 128) for layer in range(2) for half in (first, second)
    ]


def kernel(
    patch_s, split_s, gates_hbm, qkv_hbm, kv_hbm, text_hbm, ent_hbm,
    cache, att, hand,
    gates_v, qkv_v, text_v, ent_v, stage, tstage,
    send_q, send_kv, recv_q, recv_kv, keys, values, queries, send_b, recv_b,
    load_sem, q_send, q_recv, kv_send, kv_recv, e_send, e_recv, b_send, b_recv, ready_sem,
):
    sections = lax.axis_size("section")
    sec = lax.axis_index("section")
    me = lax.axis_index("seq")
    after = lax.rem(sec + 1, sections)
    before = lax.rem(sec + sections - 1, sections)

    load_qkv = pltpu.make_async_copy(qkv_hbm, qkv_v, load_sem.at[0])
    load_kv = pltpu.make_async_copy(kv_hbm, cache, load_sem.at[1])
    load_text = pltpu.make_async_copy(text_hbm, text_v, load_sem.at[2])
    load_gates = pltpu.make_async_copy(gates_hbm, gates_v, load_sem.at[3])
    load_qkv.start()

    barrier = pltpu.get_barrier_semaphore()
    for other in (after, before):
        pl.semaphore_signal(barrier, inc=1, device_id=(other, me), device_id_type=MESH)
    for flip in far_first():
        pl.semaphore_signal(
            barrier, inc=1, device_id=(sec, jnp.bitwise_xor(me, flip)), device_id_type=MESH
        )
    load_kv.start()
    load_text.start()
    load_gates.start()

    def arrange(part):
        for lg in range(LG):
            rows = qkv_v[lg * 3 + part].astype(F32)
            for at in range(4):
                stage[pl.ds(lg * 4 + at, SEQ, stride=16), :] = rows[:, at * 128:(at + 1) * 128]
        return stage[...].reshape(SEQ, 16, 128).astype(BF)

    load_qkv.wait()
    send_q[...] = arrange(0)
    pl.semaphore_wait(barrier, SEQ + 1)

    def q_copy(other):
        return pltpu.make_async_remote_copy(
            src_ref=send_q.at[other], dst_ref=recv_q.at[me], send_sem=q_send, recv_sem=q_recv,
            device_id=(sec, other), device_id_type=MESH,
        )

    def kv_copy(other):
        return pltpu.make_async_remote_copy(
            src_ref=send_kv.at[other], dst_ref=recv_kv.at[me], send_sem=kv_send, recv_sem=kv_recv,
            device_id=(sec, other), device_id_type=MESH,
        )

    def b_copy(other):
        return pltpu.make_async_remote_copy(
            src_ref=send_b.at[other], dst_ref=recv_b.at[me], send_sem=b_send, recv_sem=b_recv,
            device_id=(after, other), device_id_type=MESH,
        )

    for flip in far_first():
        q_copy(jnp.bitwise_xor(me, flip)).start()
    pltpu.make_async_copy(send_q.at[me], recv_q.at[me], q_recv).start()
    send_kv[:, :, 0:128] = arrange(1)
    send_kv[:, :, 128:256] = arrange(2)
    for flip in far_first():
        kv_copy(jnp.bitwise_xor(me, flip)).start()
    pltpu.make_async_copy(send_kv.at[me], recv_kv.at[me], kv_recv).start()
    pl.semaphore_signal(ready_sem, inc=1, device_id=(before, me), device_id_type=MESH)
    ent_copy = pltpu.make_async_remote_copy(
        src_ref=ent_hbm, dst_ref=ent_v, send_sem=e_send, recv_sem=e_recv,
        device_id=(after, me), device_id_type=MESH,
    )
    ent_copy.start()

    load_kv.wait()
    load_text.wait()
    load_gates.wait()
    slots = jnp.full((PAIRS, 128), patch_s[0], jnp.int32)
    counts = jnp.full((PAIRS, 128), split_s[0], jnp.int32)
    column = lax.broadcasted_iota(jnp.int32, (VROWS - 128, NKEY), 1)
    evens = lax.broadcasted_iota(jnp.int32, (VROWS - 128, NKEY), 0) < 8
    whole_pairs = STALE + TXT // 2
    counted = (column < whole_pairs) | ((column == whole_pairs) & evens)
    ones = jnp.where(counted, 1.0, 0.0).astype(BF)

    def prepare(lg, carry):
        tstage[...] = cache[lg].astype(F32)
        for at in range(PATCHES - 1):
            ahead = at < slots
            rows = pl.ds(at * PAIRS, PAIRS)
            here, later = at * 256, (at + 1) * 256
            keys[lg, rows, :] = jnp.where(
                ahead,
                tstage[pl.ds(here, PAIRS, stride=2), :],
                tstage[pl.ds(later, PAIRS, stride=2), :],
            ).astype(BF)
            values[lg, 0:128, rows] = jnp.where(
                ahead,
                tstage[pl.ds(here + 1, PAIRS, stride=2), :],
                tstage[pl.ds(later + 1, PAIRS, stride=2), :],
            ).T.astype(BF)
        for at in range(TXT // 2):
            tstage[2 * at:2 * at + 2, :] = text_v[lg, :, at * 128:(at + 1) * 128].astype(F32)
        last = text_v[lg, :, TXT // 2 * 128:TXT * HD].astype(F32)
        last = jnp.concatenate([last, last], axis=1)
        row = lax.broadcasted_iota(jnp.int32, (TROWS, 128), 0)
        lane = lax.broadcasted_iota(jnp.int32, (TROWS, 128), 1)
        whole = row < TXT // 2
        half = (row == TXT // 2) & (lane < HD)
        keys[lg, STALE:, :] = jnp.where(
            whole, tstage[pl.ds(0, TROWS, stride=2), :], last[0:1]
        ).astype(BF)
        end = jnp.where(half, last[1:2], 0.0)
        values[lg, 0:128, STALE:] = jnp.where(
            whole, tstage[pl.ds(1, TROWS, stride=2), :], end
        ).T.astype(BF)
        values[lg, 128:, :] = ones
        return carry

    lax.fori_loop(0, LG, prepare, 0)

    pltpu.make_async_copy(recv_q, recv_q, q_recv).wait()
    lanes = lax.broadcasted_iota(jnp.int32, (PAIRS, 128), 1) < HD
    for lg, q in enumerate(split_pieces(recv_q[...])):
        turned = pltpu.roll(q, HD, 1)
        queries[lg, 0:128] = jnp.where(lanes, q, 0.0).astype(BF)
        queries[lg, 128:256] = jnp.where(lanes, turned, 0.0).astype(BF)
        queries[lg, 256:384] = jnp.where(lanes, 0.0, turned).astype(BF)
        queries[lg, 384:512] = jnp.where(lanes, 0.0, q).astype(BF)

    def scores_of(lg, k):
        s = lax.dot_general(k, queries[lg], (((1,), (1,)), ((), ())), preferred_element_type=F32)
        best = jnp.max(s, axis=0, keepdims=True)
        return s, jnp.maximum(best[:, 0:256], best[:, 256:512])

    def twice(x):
        return jnp.concatenate([x, x], axis=1)

    old, partial = [], []
    for lg in range(LG):
        s, best = scores_of(lg, keys[lg])
        w = jnp.exp2((s - twice(best)) * FACTOR).astype(BF)
        old.append(best)
        partial.append(jnp.dot(values[lg], w, preferred_element_type=F32))

    pltpu.make_async_copy(recv_kv, recv_kv, kv_recv).wait()
    fresh_k = split_pieces(recv_kv[:, :, 0:128])
    fresh_v = split_pieces(recv_kv[:, :, 128:256])
    attended, branch = [], [None, None]
    mine = lax.broadcasted_iota(jnp.int32, (2, SEQ), 1) == me
    for lg in range(LG):
        layer, half = lg // 2, lg % 2
        s, best = scores_of(lg, fresh_k[lg].astype(BF))
        best = jnp.maximum(old[lg], best)
        w = jnp.exp2((s - twice(best)) * FACTOR).astype(BF)
        v = jnp.concatenate(
            [fresh_v[lg].T.astype(BF), jnp.ones((VROWS - 128, PAIRS), BF)], axis=0
        )
        scale = jnp.exp2((old[lg] - best) * FACTOR)
        total = jnp.dot(v, w, preferred_element_type=F32) + partial[lg] * twice(scale)

        def joined(at, low, high, size):
            cols = slice(at * 128, at * 128 + 128)
            cols2 = slice(at * 128 + 256, at * 128 + 384)
            return total[low:low + size, cols] + total[high:high + size, cols2]

        out = jnp.concatenate(
            [joined(at, 0, 64, 64) / joined(at, 128, 136, 8)[0:1] for at in range(2)], axis=0
        ).T
        out = jnp.where(layer < counts, out, 0.0).astype(BF).astype(F32)
        attended.append(out)
        gate = jnp.sum(jnp.where(mine, gates_v[layer], 0.0), axis=1, keepdims=True)
        gated = gate[half:half + 1] * out
        branch[half] = gated if branch[half] is None else branch[half] + gated

    first, second = (part.reshape(16, 8, 128) for part in branch)
    mask = low_rows(first.shape)
    even = jnp.where(mask, first, pltpu.roll(second, 4, 1))
    odd = jnp.where(mask, pltpu.roll(first, 4, 1), second)
    send_b[...] = jnp.stack([even, odd], axis=1).reshape(SEQ, 8, 128).astype(BF)
    pl.semaphore_wait(ready_sem, 1)
    for flip in far_first() + [0]:
        b_copy(jnp.bitwise_xor(me, flip)).start()

    for lg in range(LG):
        layer, half = lg // 2, lg % 2
        tstage[pl.ds(lg * 256, PAIRS, stride=2), :] = fresh_k[lg]
        tstage[pl.ds(lg * 256 + 1, PAIRS, stride=2), :] = fresh_v[lg]
        for at in range(PATCHES * 2):
            here = (layer < counts) & (slots == at // 2)
            rows = pl.ds(at * 128, 128)
            fresh = tstage[pl.ds(lg * 256 + at % 2 * 128, 128), :]
            cache[lg, rows, :] = jnp.where(here, fresh, cache[lg, rows, :].astype(F32)).astype(BF)
        stage[pl.ds(layer * 256 + half, PAIRS, stride=2), :] = attended[lg]
    att[...] = stage[...].astype(BF)

    ent_copy.wait()
    pltpu.make_async_copy(recv_b, recv_b, b_recv).wait()
    tstage[0:256, :] = recv_b[...].astype(F32).reshape(256, 128)
    for half in range(2):
        for at in range(4):
            cols = pl.ds(at * 128, 128)
            moved = tstage[pl.ds(half * 4 + at, SEQ, stride=8), :]
            hand[half, :, cols] = (ent_v[half, :, cols].astype(F32) + moved).astype(BF)

    pltpu.make_async_copy(send_b, send_b, b_send).wait()
    rest = pl.ds(0, SEQ - 1)
    pltpu.make_async_copy(send_q.at[rest], send_q.at[rest], q_send).wait()
    pltpu.make_async_copy(send_kv.at[rest], send_kv.at[rest], kv_send).wait()


def on_device(patch_qkv, kv_cache, text_kv, entering, gates, block_split, patch_index):
    qkv = jnp.transpose(patch_qkv, (0, 1, 3, 2, 4)).reshape(12, SEQ, 512)
    kv = kv_cache.reshape(LG, 2, ROWS, 128).transpose(0, 2, 1, 3).reshape(LG, 2 * ROWS, 128)
    text = text_kv.reshape(LG, 2, TXT * HD)
    ent = entering.reshape(2, SEQ, 512)
    large = [
        pltpu.with_memory_space_constraint(operand, pltpu.HBM)
        for operand in (gates, qkv, kv, text, ent)
    ]
    vmem = pltpu.VMEM
    cache, att, handed = pl.pallas_call(
        kernel,
        out_shape=[
            vmem((LG, 2 * ROWS, 128), BF),
            vmem((4 * PAIRS, 128), BF),
            vmem((2, SEQ, 512), BF),
        ],
        in_specs=[pl.BlockSpec(memory_space=pltpu.SMEM)] * 2
        + [pl.BlockSpec(memory_space=pltpu.HBM)] * 5,
        out_specs=[pl.BlockSpec(memory_space=vmem)] * 3,
        scratch_shapes=[
            vmem((2, 2, SEQ), F32),
            vmem((12, SEQ, 512), BF),
            vmem((LG, 2, TXT * HD), BF),
            vmem((2, SEQ, 512), BF),
            vmem((ROWS, 128), F32),
            vmem((2 * ROWS, 128), F32),
            vmem((SEQ, 16, 128), BF),
            vmem((SEQ, 16, 256), BF),
            vmem((SEQ, 16, 128), BF),
            vmem((SEQ, 16, 256), BF),
            vmem((LG, NKEY, 128), BF),
            vmem((LG, VROWS, NKEY), BF),
            vmem((LG, 4 * PAIRS, 128), BF),
            vmem((SEQ, 8, 128), BF),
            vmem((SEQ, 8, 128), BF),
            pltpu.SemaphoreType.DMA((4,)),
            pltpu.SemaphoreType.DMA,
            pltpu.SemaphoreType.DMA,
            pltpu.SemaphoreType.DMA,
            pltpu.SemaphoreType.DMA,
            pltpu.SemaphoreType.DMA,
            pltpu.SemaphoreType.DMA,
            pltpu.SemaphoreType.DMA,
            pltpu.SemaphoreType.DMA,
            pltpu.SemaphoreType.REGULAR,
        ],
        compiler_params=pltpu.CompilerParams(
            collective_id=0, has_side_effects=True, vmem_limit_bytes=48 * 1024 * 1024
        ),
    )(patch_index, block_split, *large)
    cache = cache.reshape(LG, ROWS, 2, 128).transpose(0, 2, 1, 3).reshape(kv_cache.shape)
    att = att.reshape(2, PAIRS, 2, 128).transpose(0, 2, 1, 3).reshape(2, 2, 1, 2 * PAIRS * HD)
    return cache, att, handed.reshape(entering.shape)


def solution(mesh):
    in_specs = (
        P("section", None, None, None, "seq"),
        P("section", None, "seq", None, None),
        P("section", None, "seq", None, None),
        P("section", None, None, "seq"),
        P("section", None, None),
        P("section"),
        P("section"),
    )
    out_specs = (
        P("section", None, "seq", None, None),
        P("section", None, "seq", None),
        P("section", None, None, "seq"),
    )
    return jax.shard_map(
        on_device, mesh=mesh, in_specs=in_specs, out_specs=out_specs, check_vma=False
    )
```

time: 38.4 us -> 30.3 us (0.79)
  Pallas kernels: 31.8 us -> 25.9 us
  local copies, waits for them, and re-layouts: 4.45 us -> 2.26 us
    pallas_call x1, Pallas kernels: 31.8 us -> 25.9 us  [on_device(): pl.pallas_call(kernel, out_shape=[vmem((LG, 2 * ROWS, 128), BF), vmem((4...]
    unnamed x7 -> x3, local copies, waits for them, and re-layouts: 4.45 us -> 2.26 us
where the time goes in v1:
time: 30.3 us; the launch traced here: 30.1 us
  Pallas kernels  25.9 us (85%)
  local copies, waits for them, and re-layouts  2.26 us (7%)
  between operations  1.93 us (6%)
    pallas_call x1, Pallas kernels, on_device(): pl.pallas_call(kernel, out_shape=[vmem((LG, 2 * ROWS, 128), BF), vmem((4...  25.9 us
    unnamed x3, local copies, waits for them, and re-layouts  2.26 us

profile of v1, /device:TPU:1, one launch (start us, length us, event | category | flops | bytes accessed | tf_op | source)
XLA Modules:
  0.0 30.1 jit_solution(3164805569151717224)
XLA Ops:
  1.9 25.9 %shard_map.94 = (bf16[4,1024,128]{2,1,0:T(8,128)(2,1)S(1)}, bf16[512,128]{1,0:T(8,128)(2,1)S(1)}, bf16[2,32,512]{2,1,0:T(8,128)(2,1)S(1)}) custom-call(s32[1]{0:T(128)S(6)} %copy.20.patch_s, s32[1]{0:T(128)S(6)} %copy.19.split_s, f32[2,2,32]{2,1,0:T(2,128)} %gates_hbm.1, bf16[12,32,512]{2,1,0:T(8,128)(2,1)} %bitcast.25, bf16[4,1024,128]{2,1,0:T(8,128)(2,1)} %bitcast.24, ...), custom_call_target="tpu_custom_call" | custom-call | tf_op jit(solution)/shard_map/pallas_call | solution.py:269
  27.9 1.0 %copy.16 = bf16[2,2,1,2,65536]{4,3,2,1,0:T(2,128)(2,1)} copy(bf16[2,2,1,2,65536]{4,3,2,1,0:T(2,128)(2,1)S(1)} %bitcast.21) | data formatting | bytes 2097152
  28.9 0.7 %copy.17 = bf16[2,2,1,16384]{3,1,2,0:T(2,128)(2,1)} copy(bf16[2,2,1,16384]{3,1,2,0:T(2,128)(2,1)S(1)} %bitcast.22) | data formatting | bytes 262144
  29.5 0.6 %copy.18 = bf16[1,2,32,512]{3,2,1,0:T(8,128)(2,1)} copy(bf16[1,2,32,512]{3,2,1,0:T(8,128)(2,1)S(1)} %bitcast.23) | data formatting | bytes 131072

commit v2 on v1

--- a/solution.py
+++ b/solution.py
@@ -41,15 +41,15 @@
     first = jnp.where(mask, even, pltpu.roll(odd, 4, 1)).reshape(16, 2, 8, 128)
     second = jnp.where(mask, pltpu.roll(even, 4, 1), odd).reshape(16, 2, 8, 128)
     return [
-        half[:, layer].reshape(PAIRS, 128) for layer in range(2) for half in (first, second)
+        inner[:, outer].reshape(PAIRS, 128) for outer in range(2) for inner in (first, second)
     ]
 
 
 def kernel(
     patch_s, split_s, gates_hbm, qkv_hbm, kv_hbm, text_hbm, ent_hbm,
-    cache, att, hand,
-    gates_v, qkv_v, text_v, ent_v, stage, tstage,
-    send_q, send_kv, recv_q, recv_kv, keys, values, queries, send_b, recv_b,
+    cache, att, recv_b, ent_v,
+    gates_v, qkv_v, text_v, stage, tstage,
+    send_q, send_kv, recv_q, recv_kv, keys, values, queries, send_b,
     load_sem, q_send, q_recv, kv_send, kv_recv, e_send, e_recv, b_send, b_recv, ready_sem,
 ):
     sections = lax.axis_size("section")
@@ -75,15 +75,15 @@
     load_text.start()
     load_gates.start()
 
-    def arrange(part):
-        for lg in range(LG):
-            rows = qkv_v[lg * 3 + part].astype(F32)
+    def arrange(parts):
+        for place, part in enumerate(parts):
+            rows = qkv_v[part].astype(F32)
             for at in range(4):
-                stage[pl.ds(lg * 4 + at, SEQ, stride=16), :] = rows[:, at * 128:(at + 1) * 128]
+                stage[pl.ds(place * 4 + at, SEQ, stride=16), :] = rows[:, at * 128:(at + 1) * 128]
         return stage[...].reshape(SEQ, 16, 128).astype(BF)
 
     load_qkv.wait()
-    send_q[...] = arrange(0)
+    send_q[...] = arrange([0, 3, 6, 9])
     pl.semaphore_wait(barrier, SEQ + 1)
 
     def q_copy(other):
@@ -92,26 +92,31 @@
             device_id=(sec, other), device_id_type=MESH,
         )
 
-    def kv_copy(other):
+    def kv_copy(half, other):
         return pltpu.make_async_remote_copy(
-            src_ref=send_kv.at[other], dst_ref=recv_kv.at[me], send_sem=kv_send, recv_sem=kv_recv,
+            src_ref=send_kv.at[half, other], dst_ref=recv_kv.at[half, me],
+            send_sem=kv_send.at[half], recv_sem=kv_recv.at[half],
             device_id=(sec, other), device_id_type=MESH,
         )
 
-    def b_copy(other):
+    def b_copy(half, other):
         return pltpu.make_async_remote_copy(
-            src_ref=send_b.at[other], dst_ref=recv_b.at[me], send_sem=b_send, recv_sem=b_recv,
+            src_ref=send_b.at[half, other], dst_ref=recv_b.at[half, me],
+            send_sem=b_send.at[half], recv_sem=b_recv.at[half],
             device_id=(after, other), device_id_type=MESH,
         )
 
     for flip in far_first():
         q_copy(jnp.bitwise_xor(me, flip)).start()
     pltpu.make_async_copy(send_q.at[me], recv_q.at[me], q_recv).start()
-    send_kv[:, :, 0:128] = arrange(1)
-    send_kv[:, :, 128:256] = arrange(2)
-    for flip in far_first():
-        kv_copy(jnp.bitwise_xor(me, flip)).start()
-    pltpu.make_async_copy(send_kv.at[me], recv_kv.at[me], kv_recv).start()
+    for half in range(2):
+        first = half * 3
+        send_kv[half] = arrange([first + 1, first + 7, first + 2, first + 8])
+        for flip in far_first():
+            kv_copy(half, jnp.bitwise_xor(me, flip)).start()
+        pltpu.make_async_copy(
+            send_kv.at[half, me], recv_kv.at[half, me], kv_recv.at[half]
+        ).start()
     pl.semaphore_signal(ready_sem, inc=1, device_id=(before, me), device_id_type=MESH)
     ent_copy = pltpu.make_async_remote_copy(
         src_ref=ent_hbm, dst_ref=ent_v, send_sem=e_send, recv_sem=e_recv,
@@ -183,26 +188,23 @@
     def twice(x):
         return jnp.concatenate([x, x], axis=1)
 
-    old, partial = [], []
-    for lg in range(LG):
+    old, partial = [None] * LG, [None] * LG
+    for lg in (0, 2, 1, 3):
         s, best = scores_of(lg, keys[lg])
         w = jnp.exp2((s - twice(best)) * FACTOR).astype(BF)
-        old.append(best)
-        partial.append(jnp.dot(values[lg], w, preferred_element_type=F32))
-
-    pltpu.make_async_copy(recv_kv, recv_kv, kv_recv).wait()
-    fresh_k = split_pieces(recv_kv[:, :, 0:128])
-    fresh_v = split_pieces(recv_kv[:, :, 128:256])
-    attended, branch = [], [None, None]
+        old[lg] = best
+        partial[lg] = jnp.dot(values[lg], w, preferred_element_type=F32)
+
     mine = lax.broadcasted_iota(jnp.int32, (2, SEQ), 1) == me
-    for lg in range(LG):
-        layer, half = lg // 2, lg % 2
-        s, best = scores_of(lg, fresh_k[lg].astype(BF))
+    gate = [
+        jnp.sum(jnp.where(mine, gates_v[layer], 0.0), axis=1, keepdims=True) for layer in range(2)
+    ]
+
+    def attend_fresh(lg, k, v):
+        s, best = scores_of(lg, k.astype(BF))
         best = jnp.maximum(old[lg], best)
         w = jnp.exp2((s - twice(best)) * FACTOR).astype(BF)
-        v = jnp.concatenate(
-            [fresh_v[lg].T.astype(BF), jnp.ones((VROWS - 128, PAIRS), BF)], axis=0
-        )
+        v = jnp.concatenate([v.T.astype(BF), jnp.ones((VROWS - 128, PAIRS), BF)], axis=0)
         scale = jnp.exp2((old[lg] - best) * FACTOR)
         total = jnp.dot(v, w, preferred_element_type=F32) + partial[lg] * twice(scale)
 
@@ -214,46 +216,65 @@
         out = jnp.concatenate(
             [joined(at, 0, 64, 64) / joined(at, 128, 136, 8)[0:1] for at in range(2)], axis=0
         ).T
-        out = jnp.where(layer < counts, out, 0.0).astype(BF).astype(F32)
-        attended.append(out)
-        gate = jnp.sum(jnp.where(mine, gates_v[layer], 0.0), axis=1, keepdims=True)
-        gated = gate[half:half + 1] * out
-        branch[half] = gated if branch[half] is None else branch[half] + gated
-
-    first, second = (part.reshape(16, 8, 128) for part in branch)
-    mask = low_rows(first.shape)
-    even = jnp.where(mask, first, pltpu.roll(second, 4, 1))
-    odd = jnp.where(mask, pltpu.roll(first, 4, 1), second)
-    send_b[...] = jnp.stack([even, odd], axis=1).reshape(SEQ, 8, 128).astype(BF)
-    pl.semaphore_wait(ready_sem, 1)
-    for flip in far_first() + [0]:
-        b_copy(jnp.bitwise_xor(me, flip)).start()
+        return jnp.where(lg // 2 < counts, out, 0.0).astype(BF).astype(F32)
+
+    fresh, attended = [None] * LG, [None] * LG
+    for half in range(2):
+        pltpu.make_async_copy(recv_kv.at[half], recv_kv.at[half], kv_recv.at[half]).wait()
+        pieces = split_pieces(recv_kv[half])
+        branch = None
+        for layer in range(2):
+            lg = layer * 2 + half
+            fresh[lg] = pieces[layer], pieces[2 + layer]
+            attended[lg] = attend_fresh(lg, *fresh[lg])
+            gated = gate[layer][half:half + 1] * attended[lg]
+            branch = gated if branch is None else branch + gated
+        send_b[half] = branch.reshape(SEQ, 4, 128).astype(BF)
+        if half == 0:
+            pl.semaphore_wait(ready_sem, 1)
+        for flip in far_first() + [0]:
+            b_copy(half, jnp.bitwise_xor(me, flip)).start()
 
     for lg in range(LG):
         layer, half = lg // 2, lg % 2
-        tstage[pl.ds(lg * 256, PAIRS, stride=2), :] = fresh_k[lg]
-        tstage[pl.ds(lg * 256 + 1, PAIRS, stride=2), :] = fresh_v[lg]
+        tstage[pl.ds(lg * 256, PAIRS, stride=2), :] = fresh[lg][0]
+        tstage[pl.ds(lg * 256 + 1, PAIRS, stride=2), :] = fresh[lg][1]
         for at in range(PATCHES * 2):
             here = (layer < counts) & (slots == at // 2)
             rows = pl.ds(at * 128, 128)
-            fresh = tstage[pl.ds(lg * 256 + at % 2 * 128, 128), :]
-            cache[lg, rows, :] = jnp.where(here, fresh, cache[lg, rows, :].astype(F32)).astype(BF)
+            new = tstage[pl.ds(lg * 256 + at % 2 * 128, 128), :]
+            cache[lg, rows, :] = jnp.where(here, new, cache[lg, rows, :].astype(F32)).astype(BF)
         stage[pl.ds(layer * 256 + half, PAIRS, stride=2), :] = attended[lg]
     att[...] = stage[...].astype(BF)
 
+    rest = pl.ds(0, SEQ - 1)
+    pltpu.make_async_copy(send_q.at[rest], send_q.at[rest], q_send).wait()
+    for half in range(2):
+        part = send_kv.at[half, rest]
+        pltpu.make_async_copy(part, part, kv_send.at[half]).wait()
     ent_copy.wait()
-    pltpu.make_async_copy(recv_b, recv_b, b_recv).wait()
-    tstage[0:256, :] = recv_b[...].astype(F32).reshape(256, 128)
-    for half in range(2):
+    for half in range(2):
+        pltpu.make_async_copy(send_b.at[half], send_b.at[half], b_send.at[half]).wait()
+        pltpu.make_async_copy(recv_b.at[half], recv_b.at[half], b_recv.at[half]).wait()
+
+
+def write_out(
+    cache, att, recv_b, ent_v, cache_hbm, att_hbm, hand_hbm, moved, hand, sem
+):
+    copies = [pltpu.make_async_copy(cache.at[lg], cache_hbm.at[lg], sem.at[lg]) for lg in range(LG)]
+    copies.append(pltpu.make_async_copy(att, att_hbm, sem.at[4]))
+    for copy in copies:
+        copy.start()
+    for half in range(2):
+        moved[...] = recv_b[half].astype(F32).reshape(PAIRS, 128)
         for at in range(4):
             cols = pl.ds(at * 128, 128)
-            moved = tstage[pl.ds(half * 4 + at, SEQ, stride=8), :]
-            hand[half, :, cols] = (ent_v[half, :, cols].astype(F32) + moved).astype(BF)
-
-    pltpu.make_async_copy(send_b, send_b, b_send).wait()
-    rest = pl.ds(0, SEQ - 1)
-    pltpu.make_async_copy(send_q.at[rest], send_q.at[rest], q_send).wait()
-    pltpu.make_async_copy(send_kv.at[rest], send_kv.at[rest], kv_send).wait()
+            branch = moved[pl.ds(at, SEQ, stride=4), :]
+            hand[half, :, cols] = (ent_v[half, :, cols].astype(F32) + branch).astype(BF)
+    copies.append(pltpu.make_async_copy(hand, hand_hbm, sem.at[5]))
+    copies[-1].start()
+    for copy in copies:
+        copy.wait()
 
 
 def on_device(patch_qkv, kv_cache, text_kv, entering, gates, block_split, patch_index):
@@ -266,47 +287,61 @@
         for operand in (gates, qkv, kv, text, ent)
     ]
     vmem = pltpu.VMEM
-    cache, att, handed = pl.pallas_call(
+    kept = pl.pallas_call(
         kernel,
         out_shape=[
             vmem((LG, 2 * ROWS, 128), BF),
             vmem((4 * PAIRS, 128), BF),
+            vmem((2, SEQ, 4, 128), BF),
             vmem((2, SEQ, 512), BF),
         ],
         in_specs=[pl.BlockSpec(memory_space=pltpu.SMEM)] * 2
         + [pl.BlockSpec(memory_space=pltpu.HBM)] * 5,
-        out_specs=[pl.BlockSpec(memory_space=vmem)] * 3,
+        out_specs=[pl.BlockSpec(memory_space=vmem)] * 4,
         scratch_shapes=[
             vmem((2, 2, SEQ), F32),
             vmem((12, SEQ, 512), BF),
             vmem((LG, 2, TXT * HD), BF),
-            vmem((2, SEQ, 512), BF),
             vmem((ROWS, 128), F32),
             vmem((2 * ROWS, 128), F32),
             vmem((SEQ, 16, 128), BF),
-            vmem((SEQ, 16, 256), BF),
+            vmem((2, SEQ, 16, 128), BF),
             vmem((SEQ, 16, 128), BF),
-            vmem((SEQ, 16, 256), BF),
+            vmem((2, SEQ, 16, 128), BF),
             vmem((LG, NKEY, 128), BF),
             vmem((LG, VROWS, NKEY), BF),
             vmem((LG, 4 * PAIRS, 128), BF),
-            vmem((SEQ, 8, 128), BF),
-            vmem((SEQ, 8, 128), BF),
+            vmem((2, SEQ, 4, 128), BF),
             pltpu.SemaphoreType.DMA((4,)),
             pltpu.SemaphoreType.DMA,
             pltpu.SemaphoreType.DMA,
+            pltpu.SemaphoreType.DMA((2,)),
+            pltpu.SemaphoreType.DMA((2,)),
             pltpu.SemaphoreType.DMA,
             pltpu.SemaphoreType.DMA,
-            pltpu.SemaphoreType.DMA,
-            pltpu.SemaphoreType.DMA,
-            pltpu.SemaphoreType.DMA,
-            pltpu.SemaphoreType.DMA,
+            pltpu.SemaphoreType.DMA((2,)),
+            pltpu.SemaphoreType.DMA((2,)),
             pltpu.SemaphoreType.REGULAR,
         ],
         compiler_params=pltpu.CompilerParams(
             collective_id=0, has_side_effects=True, vmem_limit_bytes=48 * 1024 * 1024
         ),
     )(patch_index, block_split, *large)
+    cache, att, handed = pl.pallas_call(
+        write_out,
+        out_shape=[
+            jax.ShapeDtypeStruct((LG, 2 * ROWS, 128), BF),
+            jax.ShapeDtypeStruct((4 * PAIRS, 128), BF),
+            jax.ShapeDtypeStruct((2, SEQ, 512), BF),
+        ],
+        in_specs=[pl.BlockSpec(memory_space=vmem)] * 4,
+        out_specs=[pl.BlockSpec(memory_space=pltpu.HBM)] * 3,
+        scratch_shapes=[
+            vmem((PAIRS, 128), F32),
+            vmem((2, SEQ, 512), BF),
+            pltpu.SemaphoreType.DMA((6,)),
+        ],
+    )(*[pltpu.with_memory_space_constraint(part, vmem) for part in kept])
     cache = cache.reshape(LG, ROWS, 2, 128).transpose(0, 2, 1, 3).reshape(kv_cache.shape)
     att = att.reshape(2, PAIRS, 2, 128).transpose(0, 2, 1, 3).reshape(2, 2, 1, 2 * PAIRS * HD)
     return cache, att, handed.reshape(entering.shape)

time: 30.3 us -> 29.1 us (0.960)
  local copies, waits for them, and re-layouts: 2.26 us -> 0 us
  Pallas kernels: 25.9 us -> 27.1 us
    unnamed x3 -> x0, local copies, waits for them, and re-layouts: 2.26 us -> none
    pallas_call x0 -> x1, Pallas kernels: none -> 1.07 us  [on_device(): pl.pallas_call(write_out, out_shape=[jax.ShapeDtypeStruct((LG, 2 * ROWS,...]
where the time goes in v2:
time: 29.1 us; the launch traced here: 29 us
  Pallas kernels  27.1 us (93%)
  between operations  1.93 us (7%)
    pallas_call x1, Pallas kernels, on_device(): pl.pallas_call(kernel, out_shape=[vmem((LG, 2 * ROWS, 128), BF), vmem((4...  26 us
    pallas_call x1, Pallas kernels, on_device(): pl.pallas_call(write_out, out_shape=[jax.ShapeDtypeStruct((LG, 2 * ROWS,...  1.07 us

profile of v2, /device:TPU:1, one launch (start us, length us, event | category | flops | bytes accessed | tf_op | source)
XLA Modules:
  0.0 29.0 jit_solution(6512096479675151866)
XLA Ops:
  1.9 26.0 %shard_map.94 = (bf16[4,1024,128]{2,1,0:T(8,128)(2,1)S(1)}, bf16[512,128]{1,0:T(8,128)(2,1)S(1)}, bf16[2,32,4,128]{3,2,1,0:T(4,128)(2,1)S(1)}, bf16[2,32,512]{2,1,0:T(8,128)(2,1)S(1)}) custom-call(s32[1]{0:T(128)S(6)} %copy.14.patch_s, s32[1]{0:T(128)S(6)} %copy.13.split_s, f32[2,2,32]{2,1,0:T(2,128)} %gates_hbm.1, bf16[12,32,512]{2,1,0:T(8,128)(2,1)} %bitcast.22, ...), custom_call_target="tpu_custom_call" | custom-call | tf_op jit(solution)/shard_map/pallas_call | solution.py:290
  28.0 1.1 %shard_map.95 = (bf16[4,1024,128]{2,1,0:T(8,128)(2,1)}, bf16[512,128]{1,0:T(8,128)(2,1)}, bf16[2,32,512]{2,1,0:T(8,128)(2,1)}) custom-call(bf16[4,1024,128]{2,1,0:T(8,128)(2,1)S(1)} %get-tuple-element.10.cache, bf16[512,128]{1,0:T(8,128)(2,1)S(1)} %get-tuple-element.11.att, bf16[2,32,4,128]{3,2,1,0:T(4,128)(2,1)S(1)} %get-tuple-element.12.recv_b, ...), custom_call_target="tpu_custom_call" | custom-call | tf_op jit(solution)/shard_map/pallas_call | solution.py:330

commit v3 on v2

--- a/solution.py
+++ b/solution.py
@@ -33,16 +33,13 @@
     return lax.broadcasted_iota(jnp.int32, shape, len(shape) - 2) < 4
 
 
-def split_pieces(x):
-    pieces = x.astype(F32).reshape(16, 2, 2, 8, 128)
+def split_layers(x):
+    pieces = x.astype(F32).reshape(16, 2, 8, 128)
     even, odd = pieces[:, 0], pieces[:, 1]
-    even, odd = even.reshape(32, 8, 128), odd.reshape(32, 8, 128)
     mask = low_rows(even.shape)
-    first = jnp.where(mask, even, pltpu.roll(odd, 4, 1)).reshape(16, 2, 8, 128)
-    second = jnp.where(mask, pltpu.roll(even, 4, 1), odd).reshape(16, 2, 8, 128)
-    return [
-        inner[:, outer].reshape(PAIRS, 128) for outer in range(2) for inner in (first, second)
-    ]
+    first = jnp.where(mask, even, pltpu.roll(odd, 4, 1))
+    second = jnp.where(mask, pltpu.roll(even, 4, 1), odd)
+    return first.reshape(PAIRS, 128), second.reshape(PAIRS, 128)
 
 
 def kernel(
@@ -58,11 +55,14 @@
     after = lax.rem(sec + 1, sections)
     before = lax.rem(sec + sections - 1, sections)
 
-    load_qkv = pltpu.make_async_copy(qkv_hbm, qkv_v, load_sem.at[0])
+    load_q = pltpu.make_async_copy(qkv_hbm.at[:, 0], qkv_v.at[:, 0], load_sem.at[0])
+    own_kv = pl.ds(1, 2)
+    load_own = pltpu.make_async_copy(qkv_hbm.at[:, own_kv], qkv_v.at[:, own_kv], load_sem.at[4])
     load_kv = pltpu.make_async_copy(kv_hbm, cache, load_sem.at[1])
     load_text = pltpu.make_async_copy(text_hbm, text_v, load_sem.at[2])
     load_gates = pltpu.make_async_copy(gates_hbm, gates_v, load_sem.at[3])
-    load_qkv.start()
+    load_q.start()
+    load_own.start()
 
     barrier = pltpu.get_barrier_semaphore()
     for other in (after, before):
@@ -75,20 +75,26 @@
     load_text.start()
     load_gates.start()
 
-    def arrange(parts):
-        for place, part in enumerate(parts):
-            rows = qkv_v[part].astype(F32)
+    def arrange(half, parts):
+        places = [(part, layer) for part in parts for layer in range(2)]
+        size = 4 * len(places)
+        for place, (part, layer) in enumerate(places):
+            rows = qkv_v[layer * 2 + half, part].astype(F32)
             for at in range(4):
-                stage[pl.ds(place * 4 + at, SEQ, stride=16), :] = rows[:, at * 128:(at + 1) * 128]
-        return stage[...].reshape(SEQ, 16, 128).astype(BF)
-
-    load_qkv.wait()
-    send_q[...] = arrange([0, 3, 6, 9])
+                stage[pl.ds(place * 4 + at, SEQ, stride=size), :] = (
+                    rows[:, at * 128:(at + 1) * 128]
+                )
+        return stage[0:SEQ * size].reshape(SEQ, size, 128).astype(BF)
+
+    load_q.wait()
+    for half in range(2):
+        send_q[half] = arrange(half, [0])
     pl.semaphore_wait(barrier, SEQ + 1)
 
-    def q_copy(other):
+    def q_copy(half, other):
         return pltpu.make_async_remote_copy(
-            src_ref=send_q.at[other], dst_ref=recv_q.at[me], send_sem=q_send, recv_sem=q_recv,
+            src_ref=send_q.at[half, other], dst_ref=recv_q.at[half, me],
+            send_sem=q_send.at[half], recv_sem=q_recv.at[half],
             device_id=(sec, other), device_id_type=MESH,
         )
 
@@ -106,12 +112,13 @@
             device_id=(after, other), device_id_type=MESH,
         )
 
-    for flip in far_first():
-        q_copy(jnp.bitwise_xor(me, flip)).start()
-    pltpu.make_async_copy(send_q.at[me], recv_q.at[me], q_recv).start()
-    for half in range(2):
-        first = half * 3
-        send_kv[half] = arrange([first + 1, first + 7, first + 2, first + 8])
+    for half in range(2):
+        for flip in far_first():
+            q_copy(half, jnp.bitwise_xor(me, flip)).start()
+        pltpu.make_async_copy(send_q.at[half, me], recv_q.at[half, me], q_recv.at[half]).start()
+    load_own.wait()
+    for half in range(2):
+        send_kv[half] = arrange(half, [1, 2])
         for flip in far_first():
             kv_copy(half, jnp.bitwise_xor(me, flip)).start()
         pltpu.make_async_copy(
@@ -171,14 +178,17 @@
 
     lax.fori_loop(0, LG, prepare, 0)
 
-    pltpu.make_async_copy(recv_q, recv_q, q_recv).wait()
     lanes = lax.broadcasted_iota(jnp.int32, (PAIRS, 128), 1) < HD
-    for lg, q in enumerate(split_pieces(recv_q[...])):
-        turned = pltpu.roll(q, HD, 1)
-        queries[lg, 0:128] = jnp.where(lanes, q, 0.0).astype(BF)
-        queries[lg, 128:256] = jnp.where(lanes, turned, 0.0).astype(BF)
-        queries[lg, 256:384] = jnp.where(lanes, 0.0, turned).astype(BF)
-        queries[lg, 384:512] = jnp.where(lanes, 0.0, q).astype(BF)
+
+    def place_queries(half):
+        pltpu.make_async_copy(recv_q.at[half], recv_q.at[half], q_recv.at[half]).wait()
+        for layer, q in enumerate(split_layers(recv_q[half])):
+            lg = layer * 2 + half
+            turned = pltpu.roll(q, HD, 1)
+            queries[lg, 0:128] = jnp.where(lanes, q, 0.0).astype(BF)
+            queries[lg, 128:256] = jnp.where(lanes, turned, 0.0).astype(BF)
+            queries[lg, 256:384] = jnp.where(lanes, 0.0, turned).astype(BF)
+            queries[lg, 384:512] = jnp.where(lanes, 0.0, q).astype(BF)
 
     def scores_of(lg, k):
         s = lax.dot_general(k, queries[lg], (((1,), (1,)), ((), ())), preferred_element_type=F32)
@@ -190,6 +200,8 @@
 
     old, partial = [None] * LG, [None] * LG
     for lg in (0, 2, 1, 3):
+        if lg < 2:
+            place_queries(lg)
         s, best = scores_of(lg, keys[lg])
         w = jnp.exp2((s - twice(best)) * FACTOR).astype(BF)
         old[lg] = best
@@ -221,7 +233,7 @@
     fresh, attended = [None] * LG, [None] * LG
     for half in range(2):
         pltpu.make_async_copy(recv_kv.at[half], recv_kv.at[half], kv_recv.at[half]).wait()
-        pieces = split_pieces(recv_kv[half])
+        pieces = split_layers(recv_kv[half, :, 0:8]) + split_layers(recv_kv[half, :, 8:16])
         branch = None
         for layer in range(2):
             lg = layer * 2 + half
@@ -248,8 +260,9 @@
     att[...] = stage[...].astype(BF)
 
     rest = pl.ds(0, SEQ - 1)
-    pltpu.make_async_copy(send_q.at[rest], send_q.at[rest], q_send).wait()
-    for half in range(2):
+    for half in range(2):
+        part = send_q.at[half, rest]
+        pltpu.make_async_copy(part, part, q_send.at[half]).wait()
         part = send_kv.at[half, rest]
         pltpu.make_async_copy(part, part, kv_send.at[half]).wait()
     ent_copy.wait()
@@ -278,7 +291,7 @@
 
 
 def on_device(patch_qkv, kv_cache, text_kv, entering, gates, block_split, patch_index):
-    qkv = jnp.transpose(patch_qkv, (0, 1, 3, 2, 4)).reshape(12, SEQ, 512)
+    qkv = jnp.transpose(patch_qkv, (0, 1, 3, 2, 4)).reshape(LG, 3, SEQ, 512)
     kv = kv_cache.reshape(LG, 2, ROWS, 128).transpose(0, 2, 1, 3).reshape(LG, 2 * ROWS, 128)
     text = text_kv.reshape(LG, 2, TXT * HD)
     ent = entering.reshape(2, SEQ, 512)
@@ -300,21 +313,21 @@
         out_specs=[pl.BlockSpec(memory_space=vmem)] * 4,
         scratch_shapes=[
             vmem((2, 2, SEQ), F32),
-            vmem((12, SEQ, 512), BF),
+            vmem((LG, 3, SEQ, 512), BF),
             vmem((LG, 2, TXT * HD), BF),
             vmem((ROWS, 128), F32),
             vmem((2 * ROWS, 128), F32),
-            vmem((SEQ, 16, 128), BF),
+            vmem((2, SEQ, 8, 128), BF),
             vmem((2, SEQ, 16, 128), BF),
-            vmem((SEQ, 16, 128), BF),
+            vmem((2, SEQ, 8, 128), BF),
             vmem((2, SEQ, 16, 128), BF),
             vmem((LG, NKEY, 128), BF),
             vmem((LG, VROWS, NKEY), BF),
             vmem((LG, 4 * PAIRS, 128), BF),
             vmem((2, SEQ, 4, 128), BF),
-            pltpu.SemaphoreType.DMA((4,)),
-            pltpu.SemaphoreType.DMA,
-            pltpu.SemaphoreType.DMA,
+            pltpu.SemaphoreType.DMA((5,)),
+            pltpu.SemaphoreType.DMA((2,)),
+            pltpu.SemaphoreType.DMA((2,)),
             pltpu.SemaphoreType.DMA((2,)),
             pltpu.SemaphoreType.DMA((2,)),
             pltpu.SemaphoreType.DMA,

time: 29.1 us -> 28.8 us (0.990)
  Pallas kernels: 27.1 us -> 26.8 us
    pallas_call x1, Pallas kernels: 26 us -> 25.7 us  [on_device(): pl.pallas_call(kernel, out_shape=[vmem((LG, 2 * ROWS, 128), BF), vmem((4...]
where the time goes in v3:
time: 28.8 us; the launch traced here: 28.7 us
  Pallas kernels  26.8 us (93%)
  between operations  1.93 us (7%)
    pallas_call x1, Pallas kernels, on_device(): pl.pallas_call(kernel, out_shape=[vmem((LG, 2 * ROWS, 128), BF), vmem((4...  25.7 us
    pallas_call x1, Pallas kernels, on_device(): pl.pallas_call(write_out, out_shape=[jax.ShapeDtypeStruct((LG, 2 * ROWS,...  1.07 us

profile of v3, /device:TPU:1, one launch (start us, length us, event | category | flops | bytes accessed | tf_op | source)
XLA Modules:
  0.0 28.7 jit_solution(9775622100010115401)
XLA Ops:
  1.9 25.7 %shard_map.94 = (bf16[4,1024,128]{2,1,0:T(8,128)(2,1)S(1)}, bf16[512,128]{1,0:T(8,128)(2,1)S(1)}, bf16[2,32,4,128]{3,2,1,0:T(4,128)(2,1)S(1)}, bf16[2,32,512]{2,1,0:T(8,128)(2,1)S(1)}) custom-call(s32[1]{0:T(128)S(6)} %copy.14.patch_s, s32[1]{0:T(128)S(6)} %copy.13.split_s, f32[2,2,32]{2,1,0:T(2,128)} %gates_hbm.1, bf16[4,3,32,512]{3,2,1,0:T(8,128)(2,1)} %bitcast.22, ...), custom_call_target="tpu_custom_call" | custom-call | tf_op jit(solution)/shard_map/pallas_call | solution.py:303
  27.6 1.1 %shard_map.95 = (bf16[4,1024,128]{2,1,0:T(8,128)(2,1)}, bf16[512,128]{1,0:T(8,128)(2,1)}, bf16[2,32,512]{2,1,0:T(8,128)(2,1)}) custom-call(bf16[4,1024,128]{2,1,0:T(8,128)(2,1)S(1)} %get-tuple-element.10.cache, bf16[512,128]{1,0:T(8,128)(2,1)S(1)} %get-tuple-element.11.att, bf16[2,32,4,128]{3,2,1,0:T(4,128)(2,1)S(1)} %get-tuple-element.12.recv_b, ...), custom_call_target="tpu_custom_call" | custom-call | tf_op jit(solution)/shard_map/pallas_call | solution.py:343

commit v4 on v3

--- a/solution.py
+++ b/solution.py
@@ -199,13 +199,13 @@
         return jnp.concatenate([x, x], axis=1)
 
     old, partial = [None] * LG, [None] * LG
-    for lg in (0, 2, 1, 3):
-        if lg < 2:
-            place_queries(lg)
-        s, best = scores_of(lg, keys[lg])
-        w = jnp.exp2((s - twice(best)) * FACTOR).astype(BF)
-        old[lg] = best
-        partial[lg] = jnp.dot(values[lg], w, preferred_element_type=F32)
+    for half in range(2):
+        place_queries(half)
+        pair = [scores_of(lg, keys[lg]) for lg in (half, 2 + half)]
+        for lg, (s, best) in zip((half, 2 + half), pair):
+            w = jnp.exp2((s - twice(best)) * FACTOR).astype(BF)
+            old[lg] = best
+            partial[lg] = jnp.dot(values[lg], w, preferred_element_type=F32)
 
     mine = lax.broadcasted_iota(jnp.int32, (2, SEQ), 1) == me
     gate = [

time: 28.8 us -> 28.4 us (0.986)
  Pallas kernels: 26.8 us -> 26.4 us
    pallas_call x1, Pallas kernels: 25.7 us -> 25.3 us  [on_device(): pl.pallas_call(kernel, out_shape=[vmem((LG, 2 * ROWS, 128), BF), vmem((4...]
where the time goes in v4:
time: 28.4 us; the launch traced here: 28.3 us
  Pallas kernels  26.4 us (93%)
  between operations  1.93 us (7%)
    pallas_call x1, Pallas kernels, on_device(): pl.pallas_call(kernel, out_shape=[vmem((LG, 2 * ROWS, 128), BF), vmem((4...  25.3 us
    pallas_call x1, Pallas kernels, on_device(): pl.pallas_call(write_out, out_shape=[jax.ShapeDtypeStruct((LG, 2 * ROWS,...  1.07 us

profile of v4, /device:TPU:1, one launch (start us, length us, event | category | flops | bytes accessed | tf_op | source)
XLA Modules:
  0.0 28.3 jit_solution(5954417999846491813)
XLA Ops:
  1.9 25.3 %shard_map.94 = (bf16[4,1024,128]{2,1,0:T(8,128)(2,1)S(1)}, bf16[512,128]{1,0:T(8,128)(2,1)S(1)}, bf16[2,32,4,128]{3,2,1,0:T(4,128)(2,1)S(1)}, bf16[2,32,512]{2,1,0:T(8,128)(2,1)S(1)}) custom-call(s32[1]{0:T(128)S(6)} %copy.14.patch_s, s32[1]{0:T(128)S(6)} %copy.13.split_s, f32[2,2,32]{2,1,0:T(2,128)} %gates_hbm.1, bf16[4,3,32,512]{3,2,1,0:T(8,128)(2,1)} %bitcast.22, ...), custom_call_target="tpu_custom_call" | custom-call | tf_op jit(solution)/shard_map/pallas_call | solution.py:303
  27.2 1.1 %shard_map.95 = (bf16[4,1024,128]{2,1,0:T(8,128)(2,1)}, bf16[512,128]{1,0:T(8,128)(2,1)}, bf16[2,32,512]{2,1,0:T(8,128)(2,1)}) custom-call(bf16[4,1024,128]{2,1,0:T(8,128)(2,1)S(1)} %get-tuple-element.10.cache, bf16[512,128]{1,0:T(8,128)(2,1)S(1)} %get-tuple-element.11.att, bf16[2,32,4,128]{3,2,1,0:T(4,128)(2,1)S(1)} %get-tuple-element.12.recv_b, ...), custom_call_target="tpu_custom_call" | custom-call | tf_op jit(solution)/shard_map/pallas_call | solution.py:343
